TPU v7x, 32 devices: a whole 2x2x4 slice. The times are simulated.
32 devices in a mesh: seq: 8 (over y, x, core), chan: 4 (over z).
Axes of the slice: x: 2, y: 2, z: 4, core: 2. Of those that a mesh axis runs over, the one named last changes fastest.
Arguments:
- streams: bfloat16 [3, 1024, 4096], P(None, 'seq', 'chan'), may hold values from -6 to 6
- short_taps: float32 [3, 7, 4096], P(None, None, 'chan'), may hold values from -2.5 to 2.5
- spectrum: float32 [4096, 2, 2048], P(('chan', 'seq')), may hold values from -6 to 6
- residual: bfloat16 [1024, 4096], P('seq', 'chan'), may hold values from -6 to 6
Outputs:
- output: bfloat16 [1024, 4096], P('seq', 'chan')
All inputs are finite; a program needn't handle non-finite values.
Results may differ from a plain program's by a relative error of at most 0.0056.
Values may be sent and summed in bfloat16 or wider, within the bound.
No kernel may reach another device: no remote copies, remote signals or barrier semaphores. Data moves between devices by JAX's collectives and lax.ppermute only.
A program may use at most 64 MiB of HBM per device.

v0:
```python
import functools
import math

import jax
import jax.numpy as jnp
import numpy as np
from jax import lax
from jax.experimental import pallas as pl
from jax.experimental.pallas import tpu as pltpu
from jax.sharding import PartitionSpec as P

LANES = 128
TILE = 16
VMEM_LIMIT = 16 * 1024 * 1024


def passed_along(block, axis, distance):
    devices = range(lax.axis_size(axis))
    route = [(i - distance, i) for i in devices if i - distance in devices]
    return lax.ppermute(block, axis, route)


def section_sizes(length_all):
    power = length_all.bit_length() - 1
    first = (power + 2) // 3
    second = (power - first + 1) // 2
    third = power - first - second
    result = [2**first, 2**second]
    result.append(2**third)
    return result


def matmul_high(left, right):
    return jnp.dot(left, right, precision=lax.Precision.HIGHEST, preferred_element_type=jnp.float32)


def section_high(table, values):
    return jnp.einsum(
        "ka,cab->ckb",
        table,
        values,
        precision=lax.Precision.HIGHEST,
        preferred_element_type=jnp.float32,
    )


def dft_table(order, direction):
    index = jnp.arange(order, dtype=jnp.int32)
    product = index[:, None] * index[None, :] % order
    angle = direction * 2.0 * math.pi * product.astype(jnp.float32) / order
    return (jnp.cos(angle), jnp.sin(angle))


def transform(real_part, imag_part, factors, direction):
    columns, length_now = real_part.shape
    first = factors[0]
    table_cos, table_sin = dft_table(first, direction)
    if len(factors) == 1:
        real_out = matmul_high(real_part, table_cos) - matmul_high(imag_part, table_sin)
        imag_out = matmul_high(imag_part, table_cos) + matmul_high(real_part, table_sin)
        return (real_out, imag_out)
    rest = length_now // first
    real_wide = real_part.reshape(columns, first, rest)
    if imag_part is None:
        section_real = section_high(table_cos, real_wide)
        section_imag = section_high(table_sin, real_wide)
    else:
        imag_wide = imag_part.reshape(columns, first, rest)
        section_real = section_high(table_cos, real_wide) - section_high(table_sin, imag_wide)
        section_imag = section_high(table_cos, imag_wide) + section_high(table_sin, real_wide)
    outer = jnp.arange(first, dtype=jnp.int32)[:, None]
    inner = jnp.arange(rest, dtype=jnp.int32)[None, :]
    twist = (
        direction * 2.0 * math.pi * (outer * inner % length_now).astype(jnp.float32) / length_now
    )
    twist_cos = jnp.cos(twist)[None, :, :]
    twist_sin = jnp.sin(twist)[None, :, :]
    turned_real = (section_real * twist_cos - section_imag * twist_sin).reshape(
        columns * first, rest
    )
    turned_imag = (section_real * twist_sin + section_imag * twist_cos).reshape(
        columns * first, rest
    )
    real_out, imag_out = transform(turned_real, turned_imag, factors[1:], direction)
    real_out = jnp.transpose(real_out.reshape(columns, first, rest), (0, 2, 1)).reshape(
        columns, length_now
    )
    imag_out = jnp.transpose(imag_out.reshape(columns, first, rest), (0, 2, 1)).reshape(
        columns, length_now
    )
    return (real_out, imag_out)


def long_filter(gated_rows, spectrum):
    columns, length_all = gated_rows.shape
    padded = jnp.concatenate(
        [gated_rows.astype(jnp.float32), jnp.zeros((columns, length_all), jnp.float32)], axis=1
    )
    factors = section_sizes(2 * length_all)
    freq_real, freq_imag = transform(padded, None, factors, -1.0)
    spec_real = spectrum[:, 0, :]
    spec_imag = spectrum[:, 1, :]
    prod_real = freq_real * spec_real - freq_imag * spec_imag
    prod_imag = freq_real * spec_imag + freq_imag * spec_real
    back_real, back_imag = transform(prod_real, prod_imag, factors, 1.0)
    return (back_real[:, :length_all] / (2 * length_all)).astype(jnp.bfloat16)


def local_general(streams, short_taps, spectrum, residual):
    row_count = streams.shape[1]
    channels = streams.shape[2]
    span = short_taps.shape[1] - 1
    rim_rows = passed_along(streams[:, row_count - span :, :], "seq", 1)
    extended = jnp.concatenate([rim_rows, streams], axis=1)
    total = jnp.zeros((3, row_count, channels), jnp.float32)
    for offset in range(span + 1):
        total = total + short_taps[:, offset, None, :] * extended[
            :, span - offset : span - offset + row_count, :
        ].astype(jnp.float32)
    convolved = total.astype(jnp.bfloat16)
    q_conv = convolved[0]
    k_conv = convolved[1]
    v_conv = convolved[2]
    seq_devices = lax.axis_size("seq")
    owned_count = channels // seq_devices
    length_all = row_count * seq_devices
    gated = (k_conv.astype(jnp.float32) * v_conv.astype(jnp.float32)).astype(jnp.bfloat16)
    owned = lax.all_to_all(
        gated.reshape(row_count, seq_devices, owned_count),
        "seq",
        split_axis=1,
        concat_axis=0,
        tiled=True,
    )
    gated_whole = owned.reshape(length_all, owned_count)
    filtered = jnp.transpose(long_filter(jnp.transpose(gated_whole), spectrum))
    returned = lax.all_to_all(
        filtered.reshape(length_all, 1, owned_count), "seq", split_axis=0, concat_axis=1, tiled=True
    )
    filtered_local = returned.reshape(row_count, channels)
    resid = residual.astype(jnp.float32)
    mixed = resid + jax.nn.silu(resid) * q_conv.astype(jnp.float32) * filtered_local.astype(
        jnp.float32
    )
    return mixed.astype(jnp.bfloat16)


def rounded(values):
    return values.astype(jnp.bfloat16).astype(jnp.float32)


def short_conv_rolled(rows, taps):
    later = pltpu.roll(rows, 1, 0)
    pairs = [taps(2 * i) * rows + taps(2 * i + 1) * later for i in range(3)]
    pairs.append(taps(6) * rows)
    low = pairs[0] + pltpu.roll(pairs[1], 2, 0)
    high = pairs[2] + pltpu.roll(pairs[3], 2, 0)
    return rounded(low + pltpu.roll(high, 4, 0))


def row_index(count):
    return lax.broadcasted_iota(jnp.int32, (count, LANES), 0)


def own_lanes(place_ref, k):
    return pl.ds(pl.multiple_of((place_ref[0] ^ k) * LANES, LANES), LANES)


def first_link(place_ref):
    return 2 + 2 * (place_ref[0] & 1)


def pack_block(k, v, q_last, taps, out_ref):
    rows = k.shape[0]
    row = row_index(TILE)
    gated = short_conv_rolled(k, lambda j: taps(1, j)) * short_conv_rolled(
        v, lambda j: taps(2, j)
    )
    out_ref[:TILE, :] = jnp.where(row < 6, k[:TILE], gated[:TILE]).astype(jnp.bfloat16)
    out_ref[TILE:rows, :] = gated[TILE:].astype(jnp.bfloat16)
    edge = jnp.where(row < 6, v[:TILE], v[rows - TILE :])
    edge = jnp.where((row >= 6) & (row < 10), pltpu.roll(q_last, 12, 0), edge)
    out_ref[rows : rows + TILE, :] = edge.astype(jnp.bfloat16)
    half = jnp.where(row_index(8) < 2, pltpu.roll(q_last[8:], 2, 0), k[rows - 8 :])
    out_ref[rows + TILE :, :] = jnp.concatenate([half, half], axis=0).astype(jnp.bfloat16)


def chip_order(place_ref):
    first = first_link(place_ref)
    return (0, first, 6 - first, 6)


def pack_one(place_ref, kv_ref, q_ref, taps_ref, chip, p, out_ref):
    lanes = pl.ds(pl.multiple_of(((place_ref[0] & 1) ^ p) * LANES, LANES), LANES)
    owner = own_lanes(place_ref, chip_order(place_ref)[chip] ^ p)
    pack_block(
        kv_ref[chip, 0, :, lanes].astype(jnp.float32),
        kv_ref[chip, 1, :, lanes].astype(jnp.float32),
        q_ref[:, owner].astype(jnp.float32),
        lambda s, j: taps_ref[s, j : j + 1, owner],
        out_ref,
    )


def pack_first_kernel(
    place_ref, streams_ref, taps_hbm_ref, core_ref, first_ref, kv_ref, q_ref, taps_ref, sems
):
    rows = streams_ref.shape[1]
    order = chip_order(place_ref)
    shared = [
        pltpu.make_async_copy(taps_hbm_ref, taps_ref, sems.at[4]),
        pltpu.make_async_copy(
            streams_ref.at[0, pl.ds(rows - TILE, TILE), :], q_ref, sems.at[5]
        ),
    ]
    copies = {}
    for i in (1, 0, 3, 2):
        chip = (place_ref[0] ^ order[i]) >> 1
        lanes = pl.ds(pl.multiple_of(chip * (2 * LANES), 2 * LANES), 2 * LANES)
        copies[i] = pltpu.make_async_copy(
            streams_ref.at[pl.ds(1, 2), :, lanes], kv_ref.at[i], sems.at[i]
        )
        copies[i].start()
        if i == 1:
            for copy in shared:
                copy.start()
    for copy in shared:
        copy.wait()
    for i, p, out_ref in (
        (1, 0, first_ref.at[0]),
        (1, 1, first_ref.at[1]),
        (0, 1, core_ref.at[0]),
        (3, 1, core_ref.at[1]),
    ):
        if p == 0 or i != 1:
            copies[i].wait()
        pack_one(place_ref, kv_ref, q_ref, taps_ref, i, p, out_ref)
    copies[2].wait()


def pack_second_kernel(place_ref, kv_ref, q_ref, taps_ref, second_ref, far_ref):
    for i, p, out_ref in (
        (2, 0, second_ref.at[0]),
        (2, 1, second_ref.at[1]),
        (3, 0, far_ref),
    ):
        pack_one(place_ref, kv_ref, q_ref, taps_ref, i, p, out_ref)


def pack_own_kernel(place_ref, kv_ref, q_ref, taps_ref, beside_ref, own_ref):
    pack_one(place_ref, kv_ref, q_ref, taps_ref, 0, 0, own_ref)


def spectrum_kernel(quarter, part, view_ref, beside_ref, out_ref):
    blocks = view_ref.shape[0] // (2 * LANES)
    per = quarter // LANES
    scale = 1.0 / (blocks * LANES)
    row = lax.broadcasted_iota(jnp.int32, (quarter + TILE, 2 * quarter), 0)
    col = lax.broadcasted_iota(jnp.int32, (quarter + TILE, 2 * quarter), 1)
    ahead = (col < quarter) & (row == col)
    back = (col >= quarter) & (row + col == 2 * quarter)
    turn = jnp.where(ahead | back, 1.0, 0.0).astype(jnp.bfloat16)

    def columns(part, start):
        return [
            view_ref[pl.ds(2 * (start + i) + part, LANES, stride=2 * blocks), :]
            for i in range(per)
        ]

    sign = 1.0 if part == 0 else -1.0
    heads, tails = [], []
    for m in range(4):
        start = 2 * per * m
        values = columns(part, start) + [sign * v for v in columns(part, blocks - start - per)]
        values = jnp.concatenate(values, axis=1)
        high = values.astype(jnp.bfloat16)
        low = (values - high.astype(jnp.float32)).astype(jnp.bfloat16)
        both = lax.dot_general(
            turn,
            jnp.concatenate([high, low], axis=0),
            (((1,), (1,)), ((), ())),
            preferred_element_type=jnp.float32,
        )
        folded = (both[: quarter + 8, :LANES] + both[: quarter + 8, LANES:]) * scale
        out_ref[m, :, :] = folded
        heads.append(folded[0:1])
        tails.append(folded[quarter : quarter + 1])
    for m in range(4):
        out_ref[m, 0:1, :] = 0.5 * (heads[m] + sign * heads[(4 - m) % 4])
        out_ref[m, quarter : quarter + 1, :] = 0.5 * (tails[m] + sign * tails[3 - m])


def forward_kernel(pair_ref, beside_ref, out_ref):
    out_ref[...] = pair_ref[1]


def merge_kernel(far_ref, core_ref, out_ref):
    out_ref[0] = far_ref[...]
    out_ref[1] = core_ref[1]


def received(place_ref, own, core, first, second, first_on, second_on, far):
    link = first_link(place_ref)
    blocks = [
        (0, own),
        (1, core.at[0]),
        (link, first.at[0]),
        (6 - link, second.at[0]),
        ((6 - link) ^ 1, first_on),
        (link ^ 1, second_on),
    ]
    if far is not None:
        blocks += [(6, far.at[0]), (7, far.at[1])]
    return blocks


def filter_kernel(
    place_ref,
    own_ref,
    core_ref,
    first_ref,
    second_ref,
    first_on_ref,
    second_on_ref,
    far_ref,
    taps_ref,
    real_ref,
    imag_ref,
    ahead_ref,
    back_ref,
    twist_ref,
    own_out,
    core_out,
    first_out,
    second_out,
    far_out,
    edge_ref,
    halo_ref,
    x_ref,
    z_ref,
    q_ref,
):
    shards = edge_ref.shape[0]
    rows = own_ref.shape[0] - 2 * TILE
    quarter = back_ref.shape[0]
    blocks = received(
        place_ref,
        own_ref,
        core_ref,
        first_ref,
        second_ref,
        first_on_ref,
        second_on_ref,
        far_ref,
    )
    for k, block in blocks:
        source = place_ref[0] ^ k
        start = pl.multiple_of(source * rows, rows)
        x_ref[pl.ds(start, rows), :] = block[:rows, :].astype(jnp.float32)
        edge_ref[source] = block[rows:, :].astype(jnp.float32)
    row = row_index(TILE)
    own = own_lanes(place_ref, 0)

    before = None
    for s in range(shards):
        top = x_ref[s * rows : s * rows + TILE, :]
        edge = edge_ref[s, :TILE, :]
        half = edge_ref[s, TILE : TILE + 8, :]
        if before is None:
            above_k = above_v = jnp.zeros_like(edge)
            halo = jnp.zeros_like(half)
        else:
            above_v, half_before = before
            above_k = jnp.concatenate([half_before, half_before], axis=0)
            halo = jnp.where(
                row_index(8) < 6,
                pltpu.roll(above_v, 12, 0)[:8],
                pltpu.roll(half_before, 6, 0),
            )
        k_conv = short_conv_rolled(
            jnp.where(row < 8, top, above_k), lambda j: taps_ref[1, j : j + 1, own]
        )
        v_conv = short_conv_rolled(
            jnp.where(row < 8, edge, above_v), lambda j: taps_ref[2, j : j + 1, own]
        )
        x_ref[s * rows : s * rows + TILE, :] = jnp.where(row < 6, rounded(k_conv * v_conv), top)
        halo = jnp.concatenate([halo, halo], axis=0)
        halo_ref[s] = halo.astype(jnp.bfloat16)
        before = (edge, half)

    x = jnp.concatenate(
        [x_ref[pl.ds(a, quarter, stride=4), :].astype(jnp.bfloat16) for a in range(4)], axis=1
    )
    x = jnp.concatenate([x, x], axis=0)

    def combine(real, imag, g, count):
        u = []
        for a in range(4):
            if a == 0:
                u.append((real[0], imag[0]))
                continue
            wr = jnp.broadcast_to(twist_ref[g : g + count, 2 * a : 2 * a + 1], (count, LANES))
            wi = jnp.broadcast_to(
                twist_ref[g : g + count, 2 * a + 1 : 2 * a + 2], (count, LANES)
            )
            u.append((real[a] * wr - imag[a] * wi, real[a] * wi + imag[a] * wr, wr, wi))

        def four(v, sign):
            er, ei = v[0][0] + v[2][0], v[0][1] + v[2][1]
            dr, di = v[0][0] - v[2][0], v[0][1] - v[2][1]
            pr, pi = v[1][0] + v[3][0], v[1][1] + v[3][1]
            qr, qi = v[1][0] - v[3][0], v[1][1] - v[3][1]
            if sign < 0:
                one, three = (dr + qi, di - qr), (dr - qi, di + qr)
            else:
                one, three = (dr - qi, di + qr), (dr + qi, di - qr)
            return [(er + pr, ei + pi), one, (er - pr, ei - pi), three]

        freq = four(u, -1)
        prod = []
        for m in range(4):
            hr = real_ref[m, g : g + count, :]
            hi = imag_ref[m, g : g + count, :]
            xr, xi = freq[m]
            prod.append((xr * hr - xi * hi, xr * hi + xi * hr))
        v = four(prod, 1)
        out = [v[0]]
        for a in range(1, 4):
            wr, wi = u[a][2], u[a][3]
            vr, vi = v[a]
            out.append((vr * wr + vi * wi, vi * wr - vr * wi))
        return out

    part = quarter // 2
    y = None
    for half in range(2):
        base = half * quarter
        count = quarter + half * TILE
        z_ref[base : base + count, :] = jnp.dot(
            ahead_ref[base : base + count, :], x, preferred_element_type=jnp.float32
        )
        for g in range(0, part, TILE):
            real, imag = [
                [
                    z_ref[start : start + TILE, a * LANES : (a + 1) * LANES]
                    for a in range(4)
                ]
                for start in (base + g, base + part + g)
            ]
            out = combine(real, imag, half * part + g, TILE)
            for a in range(4):
                lanes = slice(a * LANES, (a + 1) * LANES)
                for i in range(2):
                    start = base + i * part + g
                    q_ref[start : start + TILE, lanes] = out[a][i].astype(jnp.bfloat16)
        term = jnp.dot(
            back_ref[:, base : base + quarter],
            q_ref[base : base + quarter, :],
            preferred_element_type=jnp.float32,
        )
        y = term if y is None else y + term
    real = [z_ref[2 * quarter : 2 * quarter + 8, a * LANES : (a + 1) * LANES] for a in range(4)]
    last = combine(real, [jnp.zeros_like(r) for r in real], quarter, 8)

    sign = 1.0 - 2.0 * (row_index(quarter) % 2).astype(jnp.float32)
    for a in range(4):
        x_ref[pl.ds(a, quarter, stride=4), :] = (
            y[:, a * LANES : (a + 1) * LANES] + sign * last[a][0][0:1, :]
        )
    link = first_link(place_ref)
    for k, out_ref in (
        (link, first_out.at[0]),
        (link ^ 1, first_out.at[1]),
        (6 - link, second_out.at[0]),
        ((6 - link) ^ 1, second_out.at[1]),
        (6, far_out),
        (7, core_out.at[1]),
        (0, own_out),
        (1, core_out.at[0]),
    ):
        target = place_ref[0] ^ k
        start = pl.multiple_of(target * rows, rows)
        out_ref[:rows, :] = x_ref[pl.ds(start, rows), :].astype(jnp.bfloat16)
        out_ref[rows:, :] = halo_ref[target]


def silu(values):
    return values / (1.0 + jnp.exp(-values))


def gain_kernel(q_ref, taps_ref, residual_ref, out_ref):
    for c in range(out_ref.shape[1] // LANES):
        lanes = slice(c * LANES, (c + 1) * LANES)
        conv = short_conv_rolled(
            q_ref[0, :, lanes].astype(jnp.float32), lambda j: taps_ref[0, j : j + 1, lanes]
        )
        out_ref[:, lanes] = silu(residual_ref[:, lanes].astype(jnp.float32)) * conv


def mixed_block(msg, lanes, gain_ref, residual_ref, q_ref, taps_ref, out_ref):
    rows = residual_ref.shape[0]
    row = row_index(TILE)
    halo = msg[rows:, :].astype(jnp.float32)
    window = jnp.where(
        row < 8, q_ref[0, :TILE, lanes].astype(jnp.float32), halo
    )
    conv = short_conv_rolled(window, lambda j: taps_ref[0, j : j + 1, lanes])
    resid = residual_ref[:TILE, lanes].astype(jnp.float32)
    gain = jnp.where(row < 6, silu(resid) * conv, gain_ref[:TILE, lanes])
    out_ref[:TILE, :] = (resid + gain * msg[:TILE, :].astype(jnp.float32)).astype(jnp.bfloat16)
    out_ref[TILE:, :] = (
        residual_ref[TILE:, lanes].astype(jnp.float32)
        + gain_ref[TILE:, lanes] * msg[TILE:rows, :].astype(jnp.float32)
    ).astype(jnp.bfloat16)


def mix_and_store(place_ref, blocks, rest, out_ref, held, sems):
    copies = []
    for i, (k, block) in enumerate(blocks):
        lanes = own_lanes(place_ref, k)
        mixed_block(block, lanes, *rest, held.at[i])
        copy = pltpu.make_async_copy(held.at[i], out_ref.at[:, lanes], sems.at[i])
        copy.start()
        copies.append(copy)
    for copy in copies:
        copy.wait()


def mix_early_kernel(place_ref, own, core, first, second, first_on, *refs):
    rest, (out_ref, held, sems) = refs[:4], refs[4:]
    blocks = received(place_ref, own, core, first, second, first_on, None, None)[:5]
    mix_and_store(place_ref, blocks, rest, out_ref, held, sems)


def mix_late_kernel(place_ref, early_ref, second_on, far, *refs):
    rest, (out_ref, held, sems) = refs[:4], refs[4:]
    blocks = [(1 ^ first_link(place_ref), second_on), (6, far.at[0]), (7, far.at[1])]
    mix_and_store(place_ref, blocks, rest, out_ref, held, sems)


def filter_tables(quarter):
    index = np.arange(quarter)
    angle = 2.0 * np.pi * (index[:, None] * index[None, :] % (2 * quarter)) / (2 * quarter)
    alternate = np.zeros((TILE, quarter))
    alternate[0] = 1.0 - 2.0 * (index % 2)
    part = quarter // 2
    cos, sin = np.cos(angle), -np.sin(angle)
    table = np.concatenate([cos[:part], sin[:part], cos[part:], sin[part:], alternate], axis=0)
    high = table.astype(jnp.bfloat16)
    low = (table - high.astype(np.float64)).astype(jnp.bfloat16)
    ahead = np.concatenate([high, low], axis=1)
    back = np.ascontiguousarray(high[: 2 * quarter].T)
    g = np.arange(quarter + 8)[:, None]
    a = np.arange(4)[None, :]
    turn = 2.0 * np.pi * (g * a) / (8 * quarter)
    twist = np.stack([np.cos(turn), -np.sin(turn)], axis=-1).reshape(quarter + 8, 8)
    return ahead, back, twist.astype(np.float32)


def estimate(flops, moved):
    return pl.CostEstimate(flops=flops, bytes_accessed=moved, transcendentals=0)


def swap(block, partner):
    return lax.ppermute(block, "seq", [(i, partner(i)) for i in range(8)])


def arranged(kernel, name, shape, *blocks, spaces=(pltpu.VMEM, pltpu.VMEM)):
    return pl.pallas_call(
        kernel,
        in_specs=[pl.BlockSpec(memory_space=space) for space in spaces],
        out_shape=jax.ShapeDtypeStruct(shape, jnp.bfloat16),
        compiler_params=pltpu.CompilerParams(vmem_limit_bytes=VMEM_LIMIT),
        cost_estimate=estimate(1 << 10, 1 << 16),
        name=name,
    )(*blocks)


def exchanged(core, first, second, far):
    core = swap(core, lambda i: i ^ 1)
    first = swap(first, lambda i: i ^ (2 + 2 * (i & 1)))
    second = swap(second, lambda i: i ^ (4 - 2 * (i & 1)))
    merged = arranged(merge_kernel, "merge", core.shape, far, core)
    return core, first, second, swap(merged, lambda i: i ^ 6), merged


def sibling_block(pair, beside):
    return arranged(
        forward_kernel, "forward", pair.shape[1:], pair, beside, spaces=(pltpu.VMEM, pl.ANY)
    )


def local_kernels(streams, short_taps, spectrum, residual):
    rows, channels = residual.shape
    shards = lax.axis_size("seq")
    length = rows * shards
    quarter = length // 4
    params = pltpu.CompilerParams(vmem_limit_bytes=VMEM_LIMIT)
    place = lax.axis_index("seq").astype(jnp.int32).reshape(1)
    scalar = pl.BlockSpec(memory_space=pltpu.SMEM)
    vector = pl.BlockSpec(memory_space=pltpu.VMEM)
    hbm = pl.BlockSpec(memory_space=pltpu.HBM)
    half = lambda *shape: jax.ShapeDtypeStruct(shape, jnp.bfloat16)
    full = lambda *shape: jax.ShapeDtypeStruct(shape, jnp.float32)
    sent = rows + 2 * TILE
    core, first, kv, q_last, taps = pl.pallas_call(
        pack_first_kernel,
        in_specs=[scalar, hbm, hbm],
        out_shape=[
            half(2, sent, LANES),
            half(2, sent, LANES),
            half(4, 2, rows, 2 * LANES),
            half(TILE, channels),
            full(*short_taps.shape),
        ],
        scratch_shapes=[pltpu.SemaphoreType.DMA((6,))],
        compiler_params=params,
        cost_estimate=estimate(1 << 30, 1 << 20),
        name="pack_first",
    )(
        place,
        pltpu.with_memory_space_constraint(streams, pltpu.HBM),
        pltpu.with_memory_space_constraint(short_taps, pltpu.HBM),
    )
    second, far = pl.pallas_call(
        pack_second_kernel,
        in_specs=[scalar] + [vector] * 3,
        out_shape=[half(2, sent, LANES), half(sent, LANES)],
        compiler_params=params,
        cost_estimate=estimate(1 << 30, 1 << 20),
        name="pack_second",
    )(place, kv, q_last, taps)
    blocks = 2 * length // LANES
    view = jnp.transpose(spectrum.reshape(LANES, 2, blocks, LANES), (0, 2, 1, 3)).reshape(
        2 * blocks * LANES, LANES
    )
    core, first, second, far, merged = exchanged(core, first, second, far)

    def spectrum_part(part, beside):
        return pl.pallas_call(
            functools.partial(spectrum_kernel, quarter, part),
            in_specs=[vector, pl.BlockSpec(memory_space=pl.ANY)],
            out_shape=full(4, quarter + 8, LANES),
            compiler_params=params,
            cost_estimate=estimate(1 << (32 - 20 * part), 1 << 22),
            name="spectrum",
        )(view, beside)

    real = spectrum_part(0, merged)
    first_block = sibling_block(first, real)
    first_on = swap(first_block, lambda i: i ^ 1)
    second_on = swap(sibling_block(second, real), lambda i: i ^ 1)
    imag = spectrum_part(1, first_on)
    own = pl.pallas_call(
        pack_own_kernel,
        in_specs=[scalar] + [vector] * 3 + [pl.BlockSpec(memory_space=pl.ANY)],
        out_shape=half(sent, LANES),
        compiler_params=params,
        cost_estimate=estimate(1 << 22, 1 << 20),
        name="pack_own",
    )(place, kv, q_last, taps, first_block)
    ahead, back_table, twist = filter_tables(quarter)
    back = rows + TILE
    own, *sent_back = pl.pallas_call(
        filter_kernel,
        in_specs=[scalar] + [vector] * 13,
        out_shape=[half(back, LANES)] + [half(2, back, LANES)] * 3 + [half(back, LANES)],
        scratch_shapes=[
            pltpu.VMEM((shards, sent - rows, LANES), jnp.float32),
            pltpu.VMEM((shards, back - rows, LANES), jnp.bfloat16),
            pltpu.VMEM((length, LANES), jnp.float32),
            pltpu.VMEM((2 * quarter + TILE, 4 * LANES), jnp.float32),
            pltpu.VMEM((2 * quarter, 4 * LANES), jnp.bfloat16),
        ],
        compiler_params=params,
        cost_estimate=estimate(1 << 30, 1 << 22),
        name="filter",
    )(
        place,
        own,
        core,
        first,
        second,
        first_on,
        second_on,
        far,
        taps,
        real,
        imag,
        ahead,
        back_table,
        twist,
    )
    whole = lambda *shape: pl.BlockSpec(shape, lambda i: (0,) * len(shape))
    gain = pl.pallas_call(
        gain_kernel,
        grid=(1,),
        in_specs=[
            whole(1, rows, channels),
            whole(*short_taps.shape),
            whole(rows, channels),
        ],
        out_specs=whole(rows, channels),
        out_shape=full(rows, channels),
        compiler_params=params,
        cost_estimate=estimate(1 << 32, 1 << 20),
        name="gain",
    )(streams, taps, residual)
    core, first, second, far, _ = exchanged(*sent_back)
    first_on, second_on = [
        swap(sibling_block(pair, gain), lambda i: i ^ 1) for pair in (first, second)
    ]
    rest = (gain, residual, streams, taps)
    stored = dict(
        out_specs=hbm,
        out_shape=half(rows, channels),
        compiler_params=params,
        cost_estimate=estimate(1 << 20, 1 << 20),
    )
    early = pl.pallas_call(
        mix_early_kernel,
        in_specs=[scalar] + [vector] * 9,
        scratch_shapes=[
            pltpu.VMEM((5, rows, LANES), jnp.bfloat16),
            pltpu.SemaphoreType.DMA((5,)),
        ],
        name="mix_early",
        **stored,
    )(place, own, core, first, second, first_on, *rest)
    return pl.pallas_call(
        mix_late_kernel,
        in_specs=[scalar, hbm] + [vector] * 6,
        scratch_shapes=[
            pltpu.VMEM((3, rows, LANES), jnp.bfloat16),
            pltpu.SemaphoreType.DMA((3,)),
        ],
        input_output_aliases={1: 0},
        name="mix_late",
        **stored,
    )(place, early, second_on, far, *rest)


def local(streams, short_taps, spectrum, residual):
    rows, channels = residual.shape
    shards = lax.axis_size("seq")
    length = rows * shards
    fits = (
        channels == shards * LANES
        and rows % TILE == 0
        and rows >= 2 * TILE
        and length % (4 * LANES) == 0
        and length <= 2048
        and short_taps.shape[1] == 7
        and shards == 8
    )
    if fits:
        return local_kernels(streams, short_taps, spectrum, residual)
    return local_general(streams, short_taps, spectrum, residual)


def solution(mesh):
    placed = (
        P(None, "seq", "chan"),
        P(None, None, "chan"),
        P(("chan", "seq"), None, None),
        P("seq", "chan"),
    )
    return jax.shard_map(
        local, mesh=mesh, in_specs=placed, out_specs=P("seq", "chan"), check_vma=False
    )
```

profile of v0, /device:TPU:0, one launch (start us, length us, event | category | flops | bytes accessed | tf_op | source)
XLA Modules:
  0.0 21.5 jit_solution(9144018284914948944)
XLA Ops:
  0.0 1.5 %pack_first.1 = (bf16[2,160,128]{2,1,0:T(8,128)(2,1)S(1)}, bf16[2,160,128]{2,1,0:T(8,128)(2,1)S(1)}, bf16[4,2,128,256]{3,2,1,0:T(8,128)(2,1)S(1)}, bf16[16,1024]{1,0:T(8,128)(2,1)S(1)}, f32[3,7,1024]{2,1,0:T(8,128)S(1)}) custom-call(s32[1]{0:T(128)} %bitcast.place_ref, bf16[3,128,1024]{2,1,0:T(8,128)(2,1)} %refs_2_.3, f32[3,7,1024]{2,1,0:T(8,128)} %taps_hbm_ref.1), custom_call_target="tpu_custom_call" | custom-call | flops 1073741824 | bytes 1048576 | tf_op jit(solution)/shard_map/pack_first/pallas_call | solution.py:606
  1.5 0.0 copy-start.1
  1.5 3.0 %collective-permute-start = (bf16[2,160,128]{2,1,0:T(8,128)(2,1)S(1)}, bf16[2,160,128]{2,1,0:T(8,128)(2,1)S(1)}, u32[]{:S(2)}, u32[]{:S(2)}) collective-permute-start(bf16[2,160,128]{2,1,0:T(8,128)(2,1)S(1)} %get-tuple-element.20), channel_id=1, source_target_pairs={{0,8},{4,20},{8,0},{12,28},{16,24},{20,4},{24,16},{28,12},{1,9},{5... | collective-permute-start | bytes 245768 | tf_op jit(solution)/shard_map/ppermute | solution.py:565
  4.5 0.0 collective-permute-start.1
  4.5 0.3 %pack_second.1 = (bf16[2,160,128]{2,1,0:T(8,128)(2,1)S(1)}, bf16[160,128]{1,0:T(8,128)(2,1)S(1)}) custom-call(s32[1]{0:T(128)} %bitcast.place_ref, bf16[4,2,128,256]{3,2,1,0:T(8,128)(2,1)S(1)} %get-tuple-element.17.kv_ref, bf16[16,1024]{1,0:T(8,128)(2,1)S(1)} %get-tuple-element.18.q_ref, f32[3,7,1024]{2,1,0:T(8,128)S(1)} %get-tuple-element.19.taps_ref.refs_3_), custom_call_target="tpu_custom_call" | custom-call | flops 1073741824 | bytes 1048576 | tf_op jit(solution)/shard_map/pack_second/pallas_call | solution.py:625
  4.8 1.6 %collective-permute-start.2 = (bf16[2,160,128]{2,1,0:T(8,128)(2,1)S(1)}, bf16[2,160,128]{2,1,0:T(8,128)(2,1)S(1)}, u32[]{:S(2)}, u32[]{:S(2)}) collective-permute-start(bf16[2,160,128]{2,1,0:T(8,128)(2,1)S(1)} %get-tuple-element.23), channel_id=1, source_target_pairs={{0,16},{4,12},{8,24},{12,4},{16,0},{20,28},{24,8},{28,20},{1,17},{... | collective-permute-start | bytes 245768 | tf_op jit(solution)/shard_map/ppermute | solution.py:565
  6.4 0.0 collective-permute-done.1.core_ref
  6.4 1.1 %collective-permute-start.5 = (bf16[2,160,128]{2,1,0:T(8,128)(2,1)S(1)}, bf16[2,160,128]{2,1,0:T(8,128)(2,1)S(1)}, u32[]{:S(2)}, u32[]{:S(2)}) collective-permute-start(bf16[2,160,128]{2,1,0:T(8,128)(2,1)S(1)} %merge.2.beside_ref), channel_id=1, source_target_pairs={{0,24},{4,28},{8,16},{12,20},{16,8},{20,12},{24,0},{28,4},{1,25},{... | collective-permute-start | bytes 245768 | tf_op jit(solution)/shard_map/ppermute | solution.py:565
  7.5 0.9 %spectrum.2.beside_ref.real_ref = f32[4,264,128]{2,1,0:T(8,128)S(1)} custom-call(f32[4096,128]{1,0:T(8,128)S(1)} %bitcast.6, bf16[2,160,128]{2,1,0:T(8,128)(2,1)S(1)} %merge.2.beside_ref), custom_call_target="tpu_custom_call" | custom-call | flops 4294967296 | bytes 4194304 | tf_op jit(solution)/shard_map/spectrum/pallas_call | solution.py:640
  8.5 0.0 copy-start.3
  8.5 0.0 copy-start.4
  8.5 0.0 copy-start.5
  8.5 0.5 %collective-permute-start.3 = (bf16[160,128]{1,0:T(8,128)(2,1)S(1)}, bf16[160,128]{1,0:T(8,128)(2,1)S(1)}, u32[]{:S(2)}, u32[]{:S(2)}) collective-permute-start(bf16[160,128]{1,0:T(8,128)(2,1)S(1)} %forward.4.beside_ref), channel_id=1, source_target_pairs={{0,4},{4,0},{8,12},{12,8},{16,20},{20,16},{24,28},{28,24},{1,5},{5... | collective-permute-start | bytes 122888 | tf_op jit(solution)/shard_map/ppermute | solution.py:565
  9.0 0.4 %collective-permute-done.2.pair_ref.second_ref = bf16[2,160,128]{2,1,0:T(8,128)(2,1)S(1)} collective-permute-done((bf16[2,160,128]{2,1,0:T(8,128)(2,1)S(1)}, bf16[2,160,128]{2,1,0:T(8,128)(2,1)S(1)}, u32[]{:S(2)}, u32[]{:S(2)}) %collective-permute-start.2) | collective-permute-done | bytes 81952 | tf_op jit(solution)/shard_map/ppermute | solution.py:565
  9.4 0.1 pack_own.1.own_ref
  9.5 0.4 %collective-permute-done.3.beside_ref.first_on_ref = bf16[160,128]{1,0:T(8,128)(2,1)S(1)} collective-permute-done((bf16[160,128]{1,0:T(8,128)(2,1)S(1)}, bf16[160,128]{1,0:T(8,128)(2,1)S(1)}, u32[]{:S(2)}, u32[]{:S(2)}) %collective-permute-start.3) | collective-permute-done | bytes 40992 | tf_op jit(solution)/shard_map/ppermute | solution.py:565
  9.9 1.0 %spectrum.3.imag_ref = f32[4,264,128]{2,1,0:T(8,128)S(1)} custom-call(f32[4096,128]{1,0:T(8,128)S(1)} %bitcast.7, bf16[160,128]{1,0:T(8,128)(2,1)S(1)} %collective-permute-done.3.beside_ref.first_on_ref), custom_call_target="tpu_custom_call" | custom-call | flops 4096 | bytes 4194304 | tf_op jit(solution)/shard_map/spectrum/pallas_call | solution.py:640
  10.8 0.0 copy-start
  10.8 0.0 copy-start.2
  10.9 1.0 %collective-permute-done.5.far_ref = bf16[2,160,128]{2,1,0:T(8,128)(2,1)S(1)} collective-permute-done((bf16[2,160,128]{2,1,0:T(8,128)(2,1)S(1)}, bf16[2,160,128]{2,1,0:T(8,128)(2,1)S(1)}, u32[]{:S(2)}, u32[]{:S(2)}) %collective-permute-start.5) | collective-permute-done | bytes 81952 | tf_op jit(solution)/shard_map/ppermute | solution.py:565
  11.9 1.3 %filter.1 = (bf16[144,128]{1,0:T(8,128)(2,1)S(1)}, bf16[2,144,128]{2,1,0:T(8,128)(2,1)S(1)}, bf16[2,144,128]{2,1,0:T(8,128)(2,1)S(1)}, bf16[2,144,128]{2,1,0:T(8,128)(2,1)S(1)}, bf16[144,128]{1,0:T(8,128)(2,1)S(1)}) custom-call(s32[1]{0:T(128)} %bitcast.place_ref, bf16[160,128]{1,0:T(8,128)(2,1)S(1)} %pack_own.1.own_ref, ...), custom_call_target="tpu_custom_call" | custom-call | flops 1073741824 | bytes 4194304 | tf_op jit(solution)/shard_map/filter/pallas_call | solution.py:664
  13.1 0.1 collective-permute-start.6
  13.2 0.8 %collective-permute-start.7 = (bf16[2,144,128]{2,1,0:T(8,128)(2,1)S(1)}, bf16[2,144,128]{2,1,0:T(8,128)(2,1)S(1)}, u32[]{:S(2)}, u32[]{:S(2)}) collective-permute-start(bf16[2,144,128]{2,1,0:T(8,128)(2,1)S(1)} %get-tuple-element.26), channel_id=1, source_target_pairs={{0,8},{4,20},{8,0},{12,28},{16,24},{20,4},{24,16},{28,12},{1,9},{5... | collective-permute-start | bytes 221192 | tf_op jit(solution)/shard_map/ppermute | solution.py:565
  14.0 1.5 %collective-permute-start.8 = (bf16[2,144,128]{2,1,0:T(8,128)(2,1)S(1)}, bf16[2,144,128]{2,1,0:T(8,128)(2,1)S(1)}, u32[]{:S(2)}, u32[]{:S(2)}) collective-permute-start(bf16[2,144,128]{2,1,0:T(8,128)(2,1)S(1)} %get-tuple-element.27), channel_id=1, source_target_pairs={{0,16},{4,12},{8,24},{12,4},{16,0},{20,28},{24,8},{28,20},{1,17},{... | collective-permute-start | bytes 221192 | tf_op jit(solution)/shard_map/ppermute | solution.py:565
  15.4 1.4 %collective-permute-start.11 = (bf16[2,144,128]{2,1,0:T(8,128)(2,1)S(1)}, bf16[2,144,128]{2,1,0:T(8,128)(2,1)S(1)}, u32[]{:S(2)}, u32[]{:S(2)}) collective-permute-start(bf16[2,144,128]{2,1,0:T(8,128)(2,1)S(1)} %merge.3), channel_id=1, source_target_pairs={{0,24},{4,28},{8,16},{12,20},{16,8},{20,12},{24,0},{28,4},{1,25},{... | collective-permute-start | bytes 221192 | tf_op jit(solution)/shard_map/ppermute | solution.py:565
  16.8 0.5 %gain.1.beside_ref.refs_0_ = f32[128,1024]{1,0:T(8,128)S(1)} custom-call(bf16[3,128,1024]{2,1,0:T(8,128)(2,1)S(1)} %copy-done, f32[3,7,1024]{2,1,0:T(8,128)S(1)} %get-tuple-element.19.taps_ref.refs_3_, bf16[128,1024]{1,0:T(8,128)(2,1)S(1)} %copy-done.2), custom_call_target="tpu_custom_call" | custom-call | flops 4294967296 | bytes 1048576 | tf_op jit(solution)/shard_map/gain/pallas_call | solution.py:695
  17.4 1.0 %collective-permute-done.7.pair_ref.first = bf16[2,144,128]{2,1,0:T(8,128)(2,1)S(1)} collective-permute-done((bf16[2,144,128]{2,1,0:T(8,128)(2,1)S(1)}, bf16[2,144,128]{2,1,0:T(8,128)(2,1)S(1)}, u32[]{:S(2)}, u32[]{:S(2)}) %collective-permute-start.7) | collective-permute-done | bytes 73760 | tf_op jit(solution)/shard_map/ppermute | solution.py:565
  18.4 0.5 %collective-permute-start.10 = (bf16[144,128]{1,0:T(8,128)(2,1)S(1)}, bf16[144,128]{1,0:T(8,128)(2,1)S(1)}, u32[]{:S(2)}, u32[]{:S(2)}) collective-permute-start(bf16[144,128]{1,0:T(8,128)(2,1)S(1)} %forward.7), channel_id=1, source_target_pairs={{0,4},{4,0},{8,12},{12,8},{16,20},{20,16},{24,28},{28,24},{1,5},{5... | collective-permute-start | bytes 110600 | tf_op jit(solution)/shard_map/ppermute | solution.py:565
  18.9 0.7 %collective-permute-done.9.first_on = bf16[144,128]{1,0:T(8,128)(2,1)S(1)} collective-permute-done((bf16[144,128]{1,0:T(8,128)(2,1)S(1)}, bf16[144,128]{1,0:T(8,128)(2,1)S(1)}, u32[]{:S(2)}, u32[]{:S(2)}) %collective-permute-start.9) | collective-permute-done | bytes 36896 | tf_op jit(solution)/shard_map/ppermute | solution.py:565
  19.6 0.8 %mix_early.1.early_ref = bf16[128,1024]{1,0:T(8,128)(2,1)} custom-call(s32[1]{0:T(128)} %bitcast.place_ref, bf16[144,128]{1,0:T(8,128)(2,1)S(1)} %get-tuple-element.24.own, bf16[2,144,128]{2,1,0:T(8,128)(2,1)S(1)} %collective-permute-done.6.core.core_ref, bf16[2,144,128]{2,1,0:T(8,128)(2,1)S(1)} %collective-permute-done.7.pair_ref.first, ...), custom_call_target="tpu_custom_call" | custom-call | flops 1048576 | bytes 1048576 | tf_op jit(solution)/shard_map/mix_early/pallas_call | solution.py:720
  20.4 0.4 %collective-permute-done.11.far = bf16[2,144,128]{2,1,0:T(8,128)(2,1)S(1)} collective-permute-done((bf16[2,144,128]{2,1,0:T(8,128)(2,1)S(1)}, bf16[2,144,128]{2,1,0:T(8,128)(2,1)S(1)}, u32[]{:S(2)}, u32[]{:S(2)}) %collective-permute-start.11) | collective-permute-done | bytes 73760 | tf_op jit(solution)/shard_map/ppermute | solution.py:565
  20.8 0.7 %mix_late.1 = bf16[128,1024]{1,0:T(8,128)(2,1)} custom-call(s32[1]{0:T(128)} %bitcast.place_ref, bf16[128,1024]{1,0:T(8,128)(2,1)} %mix_early.1.early_ref, bf16[144,128]{1,0:T(8,128)(2,1)S(1)} %collective-permute-done.10.second_on, bf16[2,144,128]{2,1,0:T(8,128)(2,1)S(1)} %collective-permute-done.11.far, ...), custom_call_target="tpu_custom_call", output_to_operand_aliasing={{}: (1, {})} | custom-call | flops 1048576 | bytes 1048576 | tf_op jit(solution)/shard_map/mix_late/pallas_call | solution.py:730
  (19 shorter events, 0.1 us)
Async XLA Ops:
  1.5 6.0 %copy-start.1 = (f32[128,2,2048]{2,1,0:T(2,128)S(1)}, f32[128,2,2048]{2,1,0:T(2,128)}, u32[]{:S(2)}) copy-start(f32[128,2,2048]{2,1,0:T(2,128)} %param.9) | copy-start | bytes 6291460
  1.5 7.0 %collective-permute-start = (bf16[2,160,128]{2,1,0:T(8,128)(2,1)S(1)}, bf16[2,160,128]{2,1,0:T(8,128)(2,1)S(1)}, u32[]{:S(2)}, u32[]{:S(2)}) collective-permute-start(bf16[2,160,128]{2,1,0:T(8,128)(2,1)S(1)} %get-tuple-element.20), channel_id=1, source_target_pairs={{0,8},{4,20},{8,0},{12,28},{16,24},{20,4},{24,16},{28,12},{1,9},{5... | collective-permute-start | bytes 245768 | tf_op jit(solution)/shard_map/ppermute | solution.py:565
  4.5 1.9 %collective-permute-start.1 = (bf16[2,160,128]{2,1,0:T(8,128)(2,1)S(1)}, bf16[2,160,128]{2,1,0:T(8,128)(2,1)S(1)}, u32[]{:S(2)}, u32[]{:S(2)}) collective-permute-start(bf16[2,160,128]{2,1,0:T(8,128)(2,1)S(1)} %get-tuple-element.22), channel_id=1, source_target_pairs={{0,4},{4,0},{8,12},{12,8},{16,20},{20,16},{24,28},{28,24},{1,5},{5... | collective-permute-start | bytes 245768 | tf_op jit(solution)/shard_map/ppermute | solution.py:565
  4.8 4.5 %collective-permute-start.2 = (bf16[2,160,128]{2,1,0:T(8,128)(2,1)S(1)}, bf16[2,160,128]{2,1,0:T(8,128)(2,1)S(1)}, u32[]{:S(2)}, u32[]{:S(2)}) collective-permute-start(bf16[2,160,128]{2,1,0:T(8,128)(2,1)S(1)} %get-tuple-element.23), channel_id=1, source_target_pairs={{0,16},{4,12},{8,24},{12,4},{16,0},{20,28},{24,8},{28,20},{1,17},{... | collective-permute-start | bytes 245768 | tf_op jit(solution)/shard_map/ppermute | solution.py:565
  6.4 5.4 %collective-permute-start.5 = (bf16[2,160,128]{2,1,0:T(8,128)(2,1)S(1)}, bf16[2,160,128]{2,1,0:T(8,128)(2,1)S(1)}, u32[]{:S(2)}, u32[]{:S(2)}) collective-permute-start(bf16[2,160,128]{2,1,0:T(8,128)(2,1)S(1)} %merge.2.beside_ref), channel_id=1, source_target_pairs={{0,24},{4,28},{8,16},{12,20},{16,8},{20,12},{24,0},{28,4},{1,25},{... | collective-permute-start | bytes 245768 | tf_op jit(solution)/shard_map/ppermute | solution.py:565
  8.5 3.4 %copy-start.3 = (bf16[528,512]{1,0:T(8,128)(2,1)S(1)}, bf16[528,512]{1,0:T(8,128)(2,1)}, u32[]{:S(2)}) copy-start(bf16[528,512]{1,0:T(8,128)(2,1)} %constant.12.clone.ahead_ref) | copy-start | bytes 1622020
  8.5 3.3 %copy-start.4 = (bf16[256,512]{1,0:T(8,128)(2,1)S(1)}, bf16[256,512]{1,0:T(8,128)(2,1)}, u32[]{:S(2)}) copy-start(bf16[256,512]{1,0:T(8,128)(2,1)} %constant.13.clone.back_ref) | copy-start | bytes 786436
  8.5 3.3 %copy-start.5 = (f32[264,8]{1,0:T(8,128)S(1)}, f32[264,8]{1,0:T(8,128)}, u32[]{:S(2)}) copy-start(f32[264,8]{1,0:T(8,128)} %constant.14.clone.twist_ref) | copy-start | bytes 25348
  8.5 1.3 %collective-permute-start.3 = (bf16[160,128]{1,0:T(8,128)(2,1)S(1)}, bf16[160,128]{1,0:T(8,128)(2,1)S(1)}, u32[]{:S(2)}, u32[]{:S(2)}) collective-permute-start(bf16[160,128]{1,0:T(8,128)(2,1)S(1)} %forward.4.beside_ref), channel_id=1, source_target_pairs={{0,4},{4,0},{8,12},{12,8},{16,20},{20,16},{24,28},{28,24},{1,5},{5... | collective-permute-start | bytes 122888 | tf_op jit(solution)/shard_map/ppermute | solution.py:565
  9.4 1.5 %collective-permute-start.4 = (bf16[160,128]{1,0:T(8,128)(2,1)S(1)}, bf16[160,128]{1,0:T(8,128)(2,1)S(1)}, u32[]{:S(2)}, u32[]{:S(2)}) collective-permute-start(bf16[160,128]{1,0:T(8,128)(2,1)S(1)} %forward.5), channel_id=1, source_target_pairs={{0,4},{4,0},{8,12},{12,8},{16,20},{20,16},{24,28},{28,24},{1,5},{5... | collective-permute-start | bytes 122888 | tf_op jit(solution)/shard_map/ppermute | solution.py:565
  10.8 6.0 %copy-start = (bf16[3,128,1024]{2,1,0:T(8,128)(2,1)S(1)}, bf16[3,128,1024]{2,1,0:T(8,128)(2,1)}, u32[]{:S(2)}) copy-start(bf16[3,128,1024]{2,1,0:T(8,128)(2,1)} %refs_2_.3) | copy-start | bytes 2359300
  10.8 6.0 %copy-start.2 = (bf16[128,1024]{1,0:T(8,128)(2,1)S(1)}, bf16[128,1024]{1,0:T(8,128)(2,1)}, u32[]{:S(2)}) copy-start(bf16[128,1024]{1,0:T(8,128)(2,1)} %refs_1_.3) | copy-start | bytes 786436
  13.1 2.3 %collective-permute-start.6 = (bf16[2,144,128]{2,1,0:T(8,128)(2,1)S(1)}, bf16[2,144,128]{2,1,0:T(8,128)(2,1)S(1)}, u32[]{:S(2)}, u32[]{:S(2)}) collective-permute-start(bf16[2,144,128]{2,1,0:T(8,128)(2,1)S(1)} %get-tuple-element.25), channel_id=1, source_target_pairs={{0,4},{4,0},{8,12},{12,8},{16,20},{20,16},{24,28},{28,24},{1,5},{5... | collective-permute-start | bytes 221192 | tf_op jit(solution)/shard_map/ppermute | solution.py:565
  13.2 5.2 %collective-permute-start.7 = (bf16[2,144,128]{2,1,0:T(8,128)(2,1)S(1)}, bf16[2,144,128]{2,1,0:T(8,128)(2,1)S(1)}, u32[]{:S(2)}, u32[]{:S(2)}) collective-permute-start(bf16[2,144,128]{2,1,0:T(8,128)(2,1)S(1)} %get-tuple-element.26), channel_id=1, source_target_pairs={{0,8},{4,20},{8,0},{12,28},{16,24},{20,4},{24,16},{28,12},{1,9},{5... | collective-permute-start | bytes 221192 | tf_op jit(solution)/shard_map/ppermute | solution.py:565
  14.0 4.4 %collective-permute-start.8 = (bf16[2,144,128]{2,1,0:T(8,128)(2,1)S(1)}, bf16[2,144,128]{2,1,0:T(8,128)(2,1)S(1)}, u32[]{:S(2)}, u32[]{:S(2)}) collective-permute-start(bf16[2,144,128]{2,1,0:T(8,128)(2,1)S(1)} %get-tuple-element.27), channel_id=1, source_target_pairs={{0,16},{4,12},{8,24},{12,4},{16,0},{20,28},{24,8},{28,20},{1,17},{... | collective-permute-start | bytes 221192 | tf_op jit(solution)/shard_map/ppermute | solution.py:565
  15.4 5.3 %collective-permute-start.11 = (bf16[2,144,128]{2,1,0:T(8,128)(2,1)S(1)}, bf16[2,144,128]{2,1,0:T(8,128)(2,1)S(1)}, u32[]{:S(2)}, u32[]{:S(2)}) collective-permute-start(bf16[2,144,128]{2,1,0:T(8,128)(2,1)S(1)} %merge.3), channel_id=1, source_target_pairs={{0,24},{4,28},{8,16},{12,20},{16,8},{20,12},{24,0},{28,4},{1,25},{... | collective-permute-start | bytes 221192 | tf_op jit(solution)/shard_map/ppermute | solution.py:565
  18.4 1.2 %collective-permute-start.9 = (bf16[144,128]{1,0:T(8,128)(2,1)S(1)}, bf16[144,128]{1,0:T(8,128)(2,1)S(1)}, u32[]{:S(2)}, u32[]{:S(2)}) collective-permute-start(bf16[144,128]{1,0:T(8,128)(2,1)S(1)} %forward.6), channel_id=1, source_target_pairs={{0,4},{4,0},{8,12},{12,8},{16,20},{20,16},{24,28},{28,24},{1,5},{5... | collective-permute-start | bytes 110600 | tf_op jit(solution)/shard_map/ppermute | solution.py:565
  18.4 2.0 %collective-permute-start.10 = (bf16[144,128]{1,0:T(8,128)(2,1)S(1)}, bf16[144,128]{1,0:T(8,128)(2,1)S(1)}, u32[]{:S(2)}, u32[]{:S(2)}) collective-permute-start(bf16[144,128]{1,0:T(8,128)(2,1)S(1)} %forward.7), channel_id=1, source_target_pairs={{0,4},{4,0},{8,12},{12,8},{16,20},{20,16},{24,28},{28,24},{1,5},{5... | collective-permute-start | bytes 110600 | tf_op jit(solution)/shard_map/ppermute | solution.py:565
where the time goes:
time: 21.6 us; the launch traced here: 21.5 us
  starting transfers between devices  10.3 us (48%)
  Pallas kernels  7.15 us (33%)
  waiting for transfers between devices  3.8 us (18%)
    ppermute x12, starting transfers between devices, swap(): return lax.ppermute(block, 'seq', [(i, partner(i)) for i in range(8)])  10.3 us
    ppermute x12, waiting for transfers between devices, swap(): return lax.ppermute(block, 'seq', [(i, partner(i)) for i in range(8)])  3.8 us
    pallas_call x2, Pallas kernels, spectrum_part(): pl.pallas_call(functools.partial(spectrum_kernel, quarter, part), in_spec...  1.91 us
    pallas_call x1, Pallas kernels, local_kernels(): pl.pallas_call(pack_first_kernel, in_specs=[scalar, hbm, hbm], out_shape=...  1.48 us
    pallas_call x1, Pallas kernels, local_kernels(): pl.pallas_call(filter_kernel, in_specs=[scalar] + [vector] * 13, out_shap...  1.26 us
    pallas_call x1, Pallas kernels, local_kernels(): pl.pallas_call(mix_early_kernel, in_specs=[scalar] + [vector] * 9, scratc...  0.77 us
    pallas_call x1, Pallas kernels, local_kernels(): pl.pallas_call(mix_late_kernel, in_specs=[scalar, hbm] + [vector] * 6, sc...  0.71 us
    pallas_call x1, Pallas kernels, local_kernels(): pl.pallas_call(gain_kernel, grid=(1,), in_specs=[whole(1, rows, channels)...  0.55 us
  transfers between devices with their start and end apart: 12, of which 6 were waited for; matrix products, arithmetic and copies ran while one was open for 0% of the time, Pallas kernels for 17%

commit v1 on v0

--- a/solution.py
+++ b/solution.py
@@ -399,10 +399,8 @@
             if a == 0:
                 u.append((real[0], imag[0]))
                 continue
-            wr = jnp.broadcast_to(twist_ref[g : g + count, 2 * a : 2 * a + 1], (count, LANES))
-            wi = jnp.broadcast_to(
-                twist_ref[g : g + count, 2 * a + 1 : 2 * a + 2], (count, LANES)
-            )
+            wr = twist_ref[2 * a - 2, g : g + count, :]
+            wi = twist_ref[2 * a - 1, g : g + count, :]
             u.append((real[a] * wr - imag[a] * wi, real[a] * wi + imag[a] * wr, wr, wi))
 
         def four(v, sign):
@@ -554,6 +552,7 @@
     a = np.arange(4)[None, :]
     turn = 2.0 * np.pi * (g * a) / (8 * quarter)
     twist = np.stack([np.cos(turn), -np.sin(turn)], axis=-1).reshape(quarter + 8, 8)
+    twist = np.repeat(twist.T[2:, :, None], LANES, axis=2)
     return ahead, back, twist.astype(np.float32)
 
 

time: 21.6 us -> 21.6 us (level)
  no operation moved by 1% of the time
where the time goes in v1:
time: 21.6 us; the launch traced here: 21.5 us
  starting transfers between devices  10.3 us (48%)
  Pallas kernels  7.15 us (33%)
  waiting for transfers between devices  3.79 us (18%)
    ppermute x12, starting transfers between devices, swap(): return lax.ppermute(block, 'seq', [(i, partner(i)) for i in range(8)])  10.3 us
    ppermute x12, waiting for transfers between devices, swap(): return lax.ppermute(block, 'seq', [(i, partner(i)) for i in range(8)])  3.79 us
    pallas_call x2, Pallas kernels, spectrum_part(): pl.pallas_call(functools.partial(spectrum_kernel, quarter, part), in_spec...  1.92 us
    pallas_call x1, Pallas kernels, local_kernels(): pl.pallas_call(pack_first_kernel, in_specs=[scalar, hbm, hbm], out_shape=...  1.48 us
    pallas_call x1, Pallas kernels, local_kernels(): pl.pallas_call(filter_kernel, in_specs=[scalar] + [vector] * 13, out_shap...  1.25 us
    pallas_call x1, Pallas kernels, local_kernels(): pl.pallas_call(mix_early_kernel, in_specs=[scalar] + [vector] * 9, scratc...  0.77 us
    pallas_call x1, Pallas kernels, local_kernels(): pl.pallas_call(mix_late_kernel, in_specs=[scalar, hbm] + [vector] * 6, sc...  0.71 us
    pallas_call x1, Pallas kernels, local_kernels(): pl.pallas_call(gain_kernel, grid=(1,), in_specs=[whole(1, rows, channels)...  0.55 us
  transfers between devices with their start and end apart: 12, of which 6 were waited for; matrix products, arithmetic and copies ran while one was open for 0% of the time, Pallas kernels for 17%

profile of v1, /device:TPU:0, one launch (start us, length us, event | category | flops | bytes accessed | tf_op | source)
XLA Modules:
  0.0 21.5 jit_solution(1513025651132477611)
XLA Ops:
  0.0 1.5 %pack_first.1 = (bf16[2,160,128]{2,1,0:T(8,128)(2,1)S(1)}, bf16[2,160,128]{2,1,0:T(8,128)(2,1)S(1)}, bf16[4,2,128,256]{3,2,1,0:T(8,128)(2,1)S(1)}, bf16[16,1024]{1,0:T(8,128)(2,1)S(1)}, f32[3,7,1024]{2,1,0:T(8,128)S(1)}) custom-call(s32[1]{0:T(128)} %bitcast.place_ref, bf16[3,128,1024]{2,1,0:T(8,128)(2,1)} %refs_2_.3, f32[3,7,1024]{2,1,0:T(8,128)} %taps_hbm_ref.1), custom_call_target="tpu_custom_call" | custom-call | flops 1073741824 | bytes 1048576 | tf_op jit(solution)/shard_map/pack_first/pallas_call | solution.py:605
  1.5 0.0 copy-start.1
  1.5 3.0 %collective-permute-start = (bf16[2,160,128]{2,1,0:T(8,128)(2,1)S(1)}, bf16[2,160,128]{2,1,0:T(8,128)(2,1)S(1)}, u32[]{:S(2)}, u32[]{:S(2)}) collective-permute-start(bf16[2,160,128]{2,1,0:T(8,128)(2,1)S(1)} %get-tuple-element.20), channel_id=1, source_target_pairs={{0,8},{4,20},{8,0},{12,28},{16,24},{20,4},{24,16},{28,12},{1,9},{5... | collective-permute-start | bytes 245768 | tf_op jit(solution)/shard_map/ppermute | solution.py:564
  4.5 0.0 collective-permute-start.1
  4.5 0.3 %pack_second.1 = (bf16[2,160,128]{2,1,0:T(8,128)(2,1)S(1)}, bf16[160,128]{1,0:T(8,128)(2,1)S(1)}) custom-call(s32[1]{0:T(128)} %bitcast.place_ref, bf16[4,2,128,256]{3,2,1,0:T(8,128)(2,1)S(1)} %get-tuple-element.17.kv_ref, bf16[16,1024]{1,0:T(8,128)(2,1)S(1)} %get-tuple-element.18.q_ref, f32[3,7,1024]{2,1,0:T(8,128)S(1)} %get-tuple-element.19.taps_ref.refs_3_), custom_call_target="tpu_custom_call" | custom-call | flops 1073741824 | bytes 1048576 | tf_op jit(solution)/shard_map/pack_second/pallas_call | solution.py:624
  4.8 1.6 %collective-permute-start.2 = (bf16[2,160,128]{2,1,0:T(8,128)(2,1)S(1)}, bf16[2,160,128]{2,1,0:T(8,128)(2,1)S(1)}, u32[]{:S(2)}, u32[]{:S(2)}) collective-permute-start(bf16[2,160,128]{2,1,0:T(8,128)(2,1)S(1)} %get-tuple-element.23), channel_id=1, source_target_pairs={{0,16},{4,12},{8,24},{12,4},{16,0},{20,28},{24,8},{28,20},{1,17},{... | collective-permute-start | bytes 245768 | tf_op jit(solution)/shard_map/ppermute | solution.py:564
  6.4 1.1 %collective-permute-start.5 = (bf16[2,160,128]{2,1,0:T(8,128)(2,1)S(1)}, bf16[2,160,128]{2,1,0:T(8,128)(2,1)S(1)}, u32[]{:S(2)}, u32[]{:S(2)}) collective-permute-start(bf16[2,160,128]{2,1,0:T(8,128)(2,1)S(1)} %merge.2.beside_ref), channel_id=1, source_target_pairs={{0,24},{4,28},{8,16},{12,20},{16,8},{20,12},{24,0},{28,4},{1,25},{... | collective-permute-start | bytes 245768 | tf_op jit(solution)/shard_map/ppermute | solution.py:564
  7.5 1.0 %spectrum.2.beside_ref.real_ref = f32[4,264,128]{2,1,0:T(8,128)S(1)} custom-call(f32[4096,128]{1,0:T(8,128)S(1)} %bitcast.6, bf16[2,160,128]{2,1,0:T(8,128)(2,1)S(1)} %merge.2.beside_ref), custom_call_target="tpu_custom_call" | custom-call | flops 4294967296 | bytes 4194304 | tf_op jit(solution)/shard_map/spectrum/pallas_call | solution.py:639
  8.5 0.0 copy-start.3
  8.5 0.0 copy-start.4
  8.5 0.0 copy-start.5
  8.5 0.5 %collective-permute-start.3 = (bf16[160,128]{1,0:T(8,128)(2,1)S(1)}, bf16[160,128]{1,0:T(8,128)(2,1)S(1)}, u32[]{:S(2)}, u32[]{:S(2)}) collective-permute-start(bf16[160,128]{1,0:T(8,128)(2,1)S(1)} %forward.4.beside_ref), channel_id=1, source_target_pairs={{0,4},{4,0},{8,12},{12,8},{16,20},{20,16},{24,28},{28,24},{1,5},{5... | collective-permute-start | bytes 122888 | tf_op jit(solution)/shard_map/ppermute | solution.py:564
  9.0 0.3 %collective-permute-done.2.pair_ref.second_ref = bf16[2,160,128]{2,1,0:T(8,128)(2,1)S(1)} collective-permute-done((bf16[2,160,128]{2,1,0:T(8,128)(2,1)S(1)}, bf16[2,160,128]{2,1,0:T(8,128)(2,1)S(1)}, u32[]{:S(2)}, u32[]{:S(2)}) %collective-permute-start.2) | collective-permute-done | bytes 81952 | tf_op jit(solution)/shard_map/ppermute | solution.py:564
  9.4 0.0 collective-permute-start.4
  9.4 0.1 pack_own.1.own_ref
  9.5 0.4 %collective-permute-done.3.beside_ref.first_on_ref = bf16[160,128]{1,0:T(8,128)(2,1)S(1)} collective-permute-done((bf16[160,128]{1,0:T(8,128)(2,1)S(1)}, bf16[160,128]{1,0:T(8,128)(2,1)S(1)}, u32[]{:S(2)}, u32[]{:S(2)}) %collective-permute-start.3) | collective-permute-done | bytes 40992 | tf_op jit(solution)/shard_map/ppermute | solution.py:564
  9.9 1.0 %spectrum.3.imag_ref = f32[4,264,128]{2,1,0:T(8,128)S(1)} custom-call(f32[4096,128]{1,0:T(8,128)S(1)} %bitcast.7, bf16[160,128]{1,0:T(8,128)(2,1)S(1)} %collective-permute-done.3.beside_ref.first_on_ref), custom_call_target="tpu_custom_call" | custom-call | flops 4096 | bytes 4194304 | tf_op jit(solution)/shard_map/spectrum/pallas_call | solution.py:639
  10.8 0.0 copy-start
  10.9 0.0 copy-start.2
  10.9 1.0 %collective-permute-done.5.far_ref = bf16[2,160,128]{2,1,0:T(8,128)(2,1)S(1)} collective-permute-done((bf16[2,160,128]{2,1,0:T(8,128)(2,1)S(1)}, bf16[2,160,128]{2,1,0:T(8,128)(2,1)S(1)}, u32[]{:S(2)}, u32[]{:S(2)}) %collective-permute-start.5) | collective-permute-done | bytes 81952 | tf_op jit(solution)/shard_map/ppermute | solution.py:564
  11.9 1.2 %filter.1 = (bf16[144,128]{1,0:T(8,128)(2,1)S(1)}, bf16[2,144,128]{2,1,0:T(8,128)(2,1)S(1)}, bf16[2,144,128]{2,1,0:T(8,128)(2,1)S(1)}, bf16[2,144,128]{2,1,0:T(8,128)(2,1)S(1)}, bf16[144,128]{1,0:T(8,128)(2,1)S(1)}) custom-call(s32[1]{0:T(128)} %bitcast.place_ref, bf16[160,128]{1,0:T(8,128)(2,1)S(1)} %pack_own.1.own_ref, ...), custom_call_target="tpu_custom_call" | custom-call | flops 1073741824 | bytes 4194304 | tf_op jit(solution)/shard_map/filter/pallas_call | solution.py:663
  13.1 0.1 collective-permute-start.6
  13.2 0.8 %collective-permute-start.7 = (bf16[2,144,128]{2,1,0:T(8,128)(2,1)S(1)}, bf16[2,144,128]{2,1,0:T(8,128)(2,1)S(1)}, u32[]{:S(2)}, u32[]{:S(2)}) collective-permute-start(bf16[2,144,128]{2,1,0:T(8,128)(2,1)S(1)} %get-tuple-element.26), channel_id=1, source_target_pairs={{0,8},{4,20},{8,0},{12,28},{16,24},{20,4},{24,16},{28,12},{1,9},{5... | collective-permute-start | bytes 221192 | tf_op jit(solution)/shard_map/ppermute | solution.py:564
  13.9 1.5 %collective-permute-start.8 = (bf16[2,144,128]{2,1,0:T(8,128)(2,1)S(1)}, bf16[2,144,128]{2,1,0:T(8,128)(2,1)S(1)}, u32[]{:S(2)}, u32[]{:S(2)}) collective-permute-start(bf16[2,144,128]{2,1,0:T(8,128)(2,1)S(1)} %get-tuple-element.27), channel_id=1, source_target_pairs={{0,16},{4,12},{8,24},{12,4},{16,0},{20,28},{24,8},{28,20},{1,17},{... | collective-permute-start | bytes 221192 | tf_op jit(solution)/shard_map/ppermute | solution.py:564
  15.4 1.4 %collective-permute-start.11 = (bf16[2,144,128]{2,1,0:T(8,128)(2,1)S(1)}, bf16[2,144,128]{2,1,0:T(8,128)(2,1)S(1)}, u32[]{:S(2)}, u32[]{:S(2)}) collective-permute-start(bf16[2,144,128]{2,1,0:T(8,128)(2,1)S(1)} %merge.3), channel_id=1, source_target_pairs={{0,24},{4,28},{8,16},{12,20},{16,8},{20,12},{24,0},{28,4},{1,25},{... | collective-permute-start | bytes 221192 | tf_op jit(solution)/shard_map/ppermute | solution.py:564
  16.8 0.5 %gain.1.beside_ref.refs_0_ = f32[128,1024]{1,0:T(8,128)S(1)} custom-call(bf16[3,128,1024]{2,1,0:T(8,128)(2,1)S(1)} %copy-done, f32[3,7,1024]{2,1,0:T(8,128)S(1)} %get-tuple-element.19.taps_ref.refs_3_, bf16[128,1024]{1,0:T(8,128)(2,1)S(1)} %copy-done.2), custom_call_target="tpu_custom_call" | custom-call | flops 4294967296 | bytes 1048576 | tf_op jit(solution)/shard_map/gain/pallas_call | solution.py:694
  17.4 1.0 %collective-permute-done.7.pair_ref.first = bf16[2,144,128]{2,1,0:T(8,128)(2,1)S(1)} collective-permute-done((bf16[2,144,128]{2,1,0:T(8,128)(2,1)S(1)}, bf16[2,144,128]{2,1,0:T(8,128)(2,1)S(1)}, u32[]{:S(2)}, u32[]{:S(2)}) %collective-permute-start.7) | collective-permute-done | bytes 73760 | tf_op jit(solution)/shard_map/ppermute | solution.py:564
  18.4 0.5 %collective-permute-start.10 = (bf16[144,128]{1,0:T(8,128)(2,1)S(1)}, bf16[144,128]{1,0:T(8,128)(2,1)S(1)}, u32[]{:S(2)}, u32[]{:S(2)}) collective-permute-start(bf16[144,128]{1,0:T(8,128)(2,1)S(1)} %forward.7), channel_id=1, source_target_pairs={{0,4},{4,0},{8,12},{12,8},{16,20},{20,16},{24,28},{28,24},{1,5},{5... | collective-permute-start | bytes 110600 | tf_op jit(solution)/shard_map/ppermute | solution.py:564
  18.9 0.7 %collective-permute-done.9.first_on = bf16[144,128]{1,0:T(8,128)(2,1)S(1)} collective-permute-done((bf16[144,128]{1,0:T(8,128)(2,1)S(1)}, bf16[144,128]{1,0:T(8,128)(2,1)S(1)}, u32[]{:S(2)}, u32[]{:S(2)}) %collective-permute-start.9) | collective-permute-done | bytes 36896 | tf_op jit(solution)/shard_map/ppermute | solution.py:564
  19.6 0.8 %mix_early.1.early_ref = bf16[128,1024]{1,0:T(8,128)(2,1)} custom-call(s32[1]{0:T(128)} %bitcast.place_ref, bf16[144,128]{1,0:T(8,128)(2,1)S(1)} %get-tuple-element.24.own, bf16[2,144,128]{2,1,0:T(8,128)(2,1)S(1)} %collective-permute-done.6.core.core_ref, bf16[2,144,128]{2,1,0:T(8,128)(2,1)S(1)} %collective-permute-done.7.pair_ref.first, ...), custom_call_target="tpu_custom_call" | custom-call | flops 1048576 | bytes 1048576 | tf_op jit(solution)/shard_map/mix_early/pallas_call | solution.py:719
  20.3 0.4 %collective-permute-done.11.far = bf16[2,144,128]{2,1,0:T(8,128)(2,1)S(1)} collective-permute-done((bf16[2,144,128]{2,1,0:T(8,128)(2,1)S(1)}, bf16[2,144,128]{2,1,0:T(8,128)(2,1)S(1)}, u32[]{:S(2)}, u32[]{:S(2)}) %collective-permute-start.11) | collective-permute-done | bytes 73760 | tf_op jit(solution)/shard_map/ppermute | solution.py:564
  20.8 0.7 %mix_late.1 = bf16[128,1024]{1,0:T(8,128)(2,1)} custom-call(s32[1]{0:T(128)} %bitcast.place_ref, bf16[128,1024]{1,0:T(8,128)(2,1)} %mix_early.1.early_ref, bf16[144,128]{1,0:T(8,128)(2,1)S(1)} %collective-permute-done.10.second_on, bf16[2,144,128]{2,1,0:T(8,128)(2,1)S(1)} %collective-permute-done.11.far, ...), custom_call_target="tpu_custom_call", output_to_operand_aliasing={{}: (1, {})} | custom-call | flops 1048576 | bytes 1048576 | tf_op jit(solution)/shard_map/mix_late/pallas_call | solution.py:729
  (19 shorter events, 0.1 us)
Async XLA Ops:
  1.5 6.0 %copy-start.1 = (f32[128,2,2048]{2,1,0:T(2,128)S(1)}, f32[128,2,2048]{2,1,0:T(2,128)}, u32[]{:S(2)}) copy-start(f32[128,2,2048]{2,1,0:T(2,128)} %param.9) | copy-start | bytes 6291460
  1.5 7.0 %collective-permute-start = (bf16[2,160,128]{2,1,0:T(8,128)(2,1)S(1)}, bf16[2,160,128]{2,1,0:T(8,128)(2,1)S(1)}, u32[]{:S(2)}, u32[]{:S(2)}) collective-permute-start(bf16[2,160,128]{2,1,0:T(8,128)(2,1)S(1)} %get-tuple-element.20), channel_id=1, source_target_pairs={{0,8},{4,20},{8,0},{12,28},{16,24},{20,4},{24,16},{28,12},{1,9},{5... | collective-permute-start | bytes 245768 | tf_op jit(solution)/shard_map/ppermute | solution.py:564
  4.5 1.9 %collective-permute-start.1 = (bf16[2,160,128]{2,1,0:T(8,128)(2,1)S(1)}, bf16[2,160,128]{2,1,0:T(8,128)(2,1)S(1)}, u32[]{:S(2)}, u32[]{:S(2)}) collective-permute-start(bf16[2,160,128]{2,1,0:T(8,128)(2,1)S(1)} %get-tuple-element.22), channel_id=1, source_target_pairs={{0,4},{4,0},{8,12},{12,8},{16,20},{20,16},{24,28},{28,24},{1,5},{5... | collective-permute-start | bytes 245768 | tf_op jit(solution)/shard_map/ppermute | solution.py:564
  4.8 4.5 %collective-permute-start.2 = (bf16[2,160,128]{2,1,0:T(8,128)(2,1)S(1)}, bf16[2,160,128]{2,1,0:T(8,128)(2,1)S(1)}, u32[]{:S(2)}, u32[]{:S(2)}) collective-permute-start(bf16[2,160,128]{2,1,0:T(8,128)(2,1)S(1)} %get-tuple-element.23), channel_id=1, source_target_pairs={{0,16},{4,12},{8,24},{12,4},{16,0},{20,28},{24,8},{28,20},{1,17},{... | collective-permute-start | bytes 245768 | tf_op jit(solution)/shard_map/ppermute | solution.py:564
  6.4 5.4 %collective-permute-start.5 = (bf16[2,160,128]{2,1,0:T(8,128)(2,1)S(1)}, bf16[2,160,128]{2,1,0:T(8,128)(2,1)S(1)}, u32[]{:S(2)}, u32[]{:S(2)}) collective-permute-start(bf16[2,160,128]{2,1,0:T(8,128)(2,1)S(1)} %merge.2.beside_ref), channel_id=1, source_target_pairs={{0,24},{4,28},{8,16},{12,20},{16,8},{20,12},{24,0},{28,4},{1,25},{... | collective-permute-start | bytes 245768 | tf_op jit(solution)/shard_map/ppermute | solution.py:564
  8.5 3.3 %copy-start.3 = (f32[6,264,128]{2,1,0:T(8,128)S(1)}, f32[6,264,128]{2,1,0:T(8,128)}, u32[]{:S(2)}) copy-start(f32[6,264,128]{2,1,0:T(8,128)} %constant.14.clone.twist_ref) | copy-start | bytes 2433028
  8.5 3.3 %copy-start.4 = (bf16[528,512]{1,0:T(8,128)(2,1)S(1)}, bf16[528,512]{1,0:T(8,128)(2,1)}, u32[]{:S(2)}) copy-start(bf16[528,512]{1,0:T(8,128)(2,1)} %constant.12.clone.ahead_ref) | copy-start | bytes 1622020
  8.5 3.3 %copy-start.5 = (bf16[256,512]{1,0:T(8,128)(2,1)S(1)}, bf16[256,512]{1,0:T(8,128)(2,1)}, u32[]{:S(2)}) copy-start(bf16[256,512]{1,0:T(8,128)(2,1)} %constant.13.clone.back_ref) | copy-start | bytes 786436
  8.5 1.3 %collective-permute-start.3 = (bf16[160,128]{1,0:T(8,128)(2,1)S(1)}, bf16[160,128]{1,0:T(8,128)(2,1)S(1)}, u32[]{:S(2)}, u32[]{:S(2)}) collective-permute-start(bf16[160,128]{1,0:T(8,128)(2,1)S(1)} %forward.4.beside_ref), channel_id=1, source_target_pairs={{0,4},{4,0},{8,12},{12,8},{16,20},{20,16},{24,28},{28,24},{1,5},{5... | collective-permute-start | bytes 122888 | tf_op jit(solution)/shard_map/ppermute | solution.py:564
  9.4 1.5 %collective-permute-start.4 = (bf16[160,128]{1,0:T(8,128)(2,1)S(1)}, bf16[160,128]{1,0:T(8,128)(2,1)S(1)}, u32[]{:S(2)}, u32[]{:S(2)}) collective-permute-start(bf16[160,128]{1,0:T(8,128)(2,1)S(1)} %forward.5), channel_id=1, source_target_pairs={{0,4},{4,0},{8,12},{12,8},{16,20},{20,16},{24,28},{28,24},{1,5},{5... | collective-permute-start | bytes 122888 | tf_op jit(solution)/shard_map/ppermute | solution.py:564
  10.8 6.0 %copy-start = (bf16[3,128,1024]{2,1,0:T(8,128)(2,1)S(1)}, bf16[3,128,1024]{2,1,0:T(8,128)(2,1)}, u32[]{:S(2)}) copy-start(bf16[3,128,1024]{2,1,0:T(8,128)(2,1)} %refs_2_.3) | copy-start | bytes 2359300
  10.9 6.0 %copy-start.2 = (bf16[128,1024]{1,0:T(8,128)(2,1)S(1)}, bf16[128,1024]{1,0:T(8,128)(2,1)}, u32[]{:S(2)}) copy-start(bf16[128,1024]{1,0:T(8,128)(2,1)} %refs_1_.3) | copy-start | bytes 786436
  13.1 2.3 %collective-permute-start.6 = (bf16[2,144,128]{2,1,0:T(8,128)(2,1)S(1)}, bf16[2,144,128]{2,1,0:T(8,128)(2,1)S(1)}, u32[]{:S(2)}, u32[]{:S(2)}) collective-permute-start(bf16[2,144,128]{2,1,0:T(8,128)(2,1)S(1)} %get-tuple-element.25), channel_id=1, source_target_pairs={{0,4},{4,0},{8,12},{12,8},{16,20},{20,16},{24,28},{28,24},{1,5},{5... | collective-permute-start | bytes 221192 | tf_op jit(solution)/shard_map/ppermute | solution.py:564
  13.2 5.2 %collective-permute-start.7 = (bf16[2,144,128]{2,1,0:T(8,128)(2,1)S(1)}, bf16[2,144,128]{2,1,0:T(8,128)(2,1)S(1)}, u32[]{:S(2)}, u32[]{:S(2)}) collective-permute-start(bf16[2,144,128]{2,1,0:T(8,128)(2,1)S(1)} %get-tuple-element.26), channel_id=1, source_target_pairs={{0,8},{4,20},{8,0},{12,28},{16,24},{20,4},{24,16},{28,12},{1,9},{5... | collective-permute-start | bytes 221192 | tf_op jit(solution)/shard_map/ppermute | solution.py:564
  13.9 4.4 %collective-permute-start.8 = (bf16[2,144,128]{2,1,0:T(8,128)(2,1)S(1)}, bf16[2,144,128]{2,1,0:T(8,128)(2,1)S(1)}, u32[]{:S(2)}, u32[]{:S(2)}) collective-permute-start(bf16[2,144,128]{2,1,0:T(8,128)(2,1)S(1)} %get-tuple-element.27), channel_id=1, source_target_pairs={{0,16},{4,12},{8,24},{12,4},{16,0},{20,28},{24,8},{28,20},{1,17},{... | collective-permute-start | bytes 221192 | tf_op jit(solution)/shard_map/ppermute | solution.py:564
  15.4 5.3 %collective-permute-start.11 = (bf16[2,144,128]{2,1,0:T(8,128)(2,1)S(1)}, bf16[2,144,128]{2,1,0:T(8,128)(2,1)S(1)}, u32[]{:S(2)}, u32[]{:S(2)}) collective-permute-start(bf16[2,144,128]{2,1,0:T(8,128)(2,1)S(1)} %merge.3), channel_id=1, source_target_pairs={{0,24},{4,28},{8,16},{12,20},{16,8},{20,12},{24,0},{28,4},{1,25},{... | collective-permute-start | bytes 221192 | tf_op jit(solution)/shard_map/ppermute | solution.py:564
  18.3 1.2 %collective-permute-start.9 = (bf16[144,128]{1,0:T(8,128)(2,1)S(1)}, bf16[144,128]{1,0:T(8,128)(2,1)S(1)}, u32[]{:S(2)}, u32[]{:S(2)}) collective-permute-start(bf16[144,128]{1,0:T(8,128)(2,1)S(1)} %forward.6), channel_id=1, source_target_pairs={{0,4},{4,0},{8,12},{12,8},{16,20},{20,16},{24,28},{28,24},{1,5},{5... | collective-permute-start | bytes 110600 | tf_op jit(solution)/shard_map/ppermute | solution.py:564
  18.4 2.0 %collective-permute-start.10 = (bf16[144,128]{1,0:T(8,128)(2,1)S(1)}, bf16[144,128]{1,0:T(8,128)(2,1)S(1)}, u32[]{:S(2)}, u32[]{:S(2)}) collective-permute-start(bf16[144,128]{1,0:T(8,128)(2,1)S(1)} %forward.7), channel_id=1, source_target_pairs={{0,4},{4,0},{8,12},{12,8},{16,20},{20,16},{24,28},{28,24},{1,5},{5... | collective-permute-start | bytes 110600 | tf_op jit(solution)/shard_map/ppermute | solution.py:564
